TPU v7x, 256 devices: a whole 4x4x8 slice. The times are simulated.
256 devices in a mesh: expert: 64 (over x, z, core), tensor: 4 (over y).
Axes of the slice: x: 4, y: 4, z: 8, core: 2. Of those that a mesh axis runs over, the one named last changes fastest.
Arguments:
- member_weights: bfloat16 [128, 3072, 2560], P('expert', 'tensor'), may hold values from -0.109375 to 0.109375
- cluster_ids: int32 [128], replicated, may hold values from 0 to 63, as said below
- merge_counts: int32 [128], replicated, may hold values from 1 to 8
- tokens: bfloat16 [4096, 3072], P('expert'), may hold values from -6 to 6
- routes: int32 [4096, 8], P('expert'), may hold values from 0 to 63, all different within a row; in each aligned block of 64 rows (0 to 63, 64 to 127, ...) at most 16 rows name the same one
Outputs:
- merged_gate_up: bfloat16 [64, 3072, 2560], P('expert', None, 'tensor')
- hidden: bfloat16 [4096, 8, 1280], P('expert', None, 'tensor')
Inputs may be any that keep to these rules, and one draw needn't show every extreme that they name: `cluster_ids`: every one of the 64 merged experts has 1 to 4 members, and some merged expert has exactly 4. `routes`: within the 64 rows of one index of expert no merged expert is named more than 16 times, and one is named exactly 16 times.
All inputs are finite; a program needn't handle non-finite values.
Results may differ from a plain program's by a relative error of at most 0.0031.
Values may be sent and summed in bfloat16 or wider, within the bound.
A program may use at most 128 MiB of HBM per device.

v0:
```python
import jax
import jax.numpy as jnp
from jax import lax
from jax.sharding import PartitionSpec as P


def on_device(member_weights, cluster_ids, merge_counts, tokens, routes):
    expert_count = lax.axis_size("expert")
    tensor_count = lax.axis_size("tensor")
    member_count = cluster_ids.shape[0]
    local_members, local_rows, united_width = member_weights.shape
    column_part = united_width // (2 * tensor_count)
    model_width = tokens.shape[1]
    cluster_range = jnp.arange(expert_count, dtype=jnp.int32)
    membership = cluster_ids[None, :] == cluster_range[:, None]
    weighted = jnp.where(membership, merge_counts[None, :], 0)
    totals = jnp.sum(weighted, axis=1).astype(jnp.float32)
    weight_table = weighted.astype(jnp.bfloat16)
    split_columns = member_weights.reshape(local_members, local_rows, 2, tensor_count, column_part)
    moved = lax.all_to_all(split_columns, "tensor", split_axis=3, concat_axis=1, tiled=True)
    full_rows = moved.reshape(local_members, local_rows * tensor_count, 2 * column_part)
    gathered = lax.all_to_all(full_rows, "expert", split_axis=1, concat_axis=0, tiled=True)
    flattened = gathered.reshape(member_count, -1)
    summed = jnp.dot(weight_table, flattened, preferred_element_type=jnp.float32) / totals[:, None]
    merged_rows = summed.astype(jnp.bfloat16).reshape((expert_count,) + gathered.shape[1:])
    owned = lax.all_to_all(merged_rows, "expert", split_axis=0, concat_axis=1, tiled=True)
    token_count, top_count = routes.shape
    capacity = max(token_count // 4, token_count * top_count // expert_count)
    flat_routes = routes.reshape(-1)
    hits = (flat_routes[:, None] == cluster_range[None, :]).astype(jnp.int32)
    earlier = jnp.cumsum(hits, axis=0) - hits
    ranking = jnp.sum(earlier * hits, axis=1)
    slot_index = flat_routes * capacity + ranking
    slot_range = jnp.arange(expert_count * capacity, dtype=jnp.int32)
    matching = (slot_range[:, None] == slot_index[None, :]).reshape(
        expert_count * capacity, token_count, top_count
    )
    selection = jnp.any(matching, axis=2).astype(jnp.bfloat16)
    outgoing = jnp.dot(selection, tokens, preferred_element_type=jnp.float32).astype(jnp.bfloat16)
    outgoing = outgoing.reshape(expert_count, capacity, tokens.shape[1])
    weights_here = owned[0]
    arrived = lax.all_to_all(outgoing, "expert", split_axis=0, concat_axis=0, tiled=True)
    item_count = arrived.shape[1]
    projected = jnp.dot(
        arrived.reshape(-1, model_width), weights_here, preferred_element_type=jnp.float32
    )
    activated = (jax.nn.silu(projected[:, :column_part]) * projected[:, column_part:]).astype(
        jnp.bfloat16
    )
    activated = activated.reshape(expert_count, item_count, column_part)
    returned = lax.all_to_all(activated, "expert", split_axis=0, concat_axis=0, tiled=True)
    hidden = returned.reshape(expert_count * capacity, column_part)[slot_index]
    return (owned, hidden.reshape(token_count, top_count, column_part))


def solution(mesh):
    return jax.shard_map(
        on_device,
        mesh=mesh,
        in_specs=(P("expert", "tensor", None), P(), P(), P("expert", None), P("expert", None)),
        out_specs=(P("expert", None, "tensor"), P("expert", None, "tensor")),
        check_vma=False,
    )
```

profile of v0, /device:TPU:1, one launch (start us, length us, event | category | flops | bytes accessed | tf_op | source)
XLA Modules:
  0.0 633.2 jit_solution(10699303026428462657)
XLA Ops:
  0.6 10.7 %copy.37 = bf16[2,768,2560]{1,2,0:T(8,128)(2,1)} copy(bf16[2,768,2560]{2,1,0:T(8,128)(2,1)} %param.5) | data formatting | bytes 15728640 | tf_op args[0]
  11.3 3.7 copy.38
  15.1 90.8 %all_to_all.52 = bf16[2,768,2,4,320]{1,4,2,0,3:T(8,128)(2,1)} all-to-all(bf16[2,768,2,4,320]{1,4,2,0,3:T(8,128)(2,1)S(1)} %copy.38), channel_id=1, replica_groups=mesh['expert'=64,'tensor'=4] {'tensor'}, dimensions={3} | all-to-all | bytes 15728640 | tf_op jit(solution)/shard_map/all_to_all | solution.py:20
  105.8 23.7 %copy.48 = bf16[2,4,768,2,1,320]{5,3,0,2,1,4:T(2,128)(2,1)} copy(bf16[2,4,768,2,1,320]{2,5,3,0,1,4:T(8,128)(2,1)} %bitcast.48) | data formatting | bytes 15728640 | tf_op jit(solution)/shard_map/reshape | solution.py:21
  129.5 25.4 %reshape.123 = bf16[2,3072,640]{2,0,1:T(2,128)(2,1)} reshape(bf16[2,4,768,2,1,320]{5,3,0,2,1,4:T(2,128)(2,1)} %copy.48) | data formatting | bytes 15728640 | tf_op jit(solution)/shard_map/reshape | solution.py:21
  154.9 15.0 %all-to-all-start.1 = ((bf16[2,3072,640]{2,0,1:T(2,128)(2,1)}), bf16[2,3072,640]{2,0,1:T(2,128)(2,1)}, u32[]{:S(2)}, u32[]{:S(2)}) async-start(bf16[2,3072,640]{2,0,1:T(2,128)(2,1)} %reshape.123), calls=%async_computation.1 | async-start | bytes 15728640 | tf_op jit(solution)/shard_map/all_to_all | solution.py:22
  170.1 0.1 eq.56
  170.2 0.1 eq.60
  170.3 1.2 reduce-window.6
  171.5 0.2 slice_reduce_fusion
  171.7 0.1 fusion.5
  171.9 0.1 reduce_sum.24
  172.0 0.7 fusion.1
  172.7 4.5 convolution_convert_fusion
  177.2 167.4 %all-to-all-done.1 = bf16[2,3072,640]{2,0,1:T(2,128)(2,1)} async-done(((bf16[2,3072,640]{2,0,1:T(2,128)(2,1)}), bf16[2,3072,640]{2,0,1:T(2,128)(2,1)}, u32[]{:S(2)}, u32[]{:S(2)}) %all-to-all-start.1) | async-done | bytes 7864352 | tf_op jit(solution)/shard_map/all_to_all | solution.py:22
  344.5 6.1 all-to-all-start.3
  350.6 0.1 select_reduce_fusion
  350.8 4.2 copy.41
  355.0 3.8 copy.42
  358.8 5.3 copy.51
  364.2 1.2 fusion
  365.4 2.5 copy.52
  367.8 123.6 %all-to-all-done.3 = bf16[64,16,3072]{2,1,0:T(8,128)(2,1)} async-done(((bf16[64,16,3072]{2,1,0:T(8,128)(2,1)}), bf16[64,16,3072]{2,1,0:T(8,128)(2,1)}, u32[]{:S(2)}, u32[]{:S(2)}) %all-to-all-start.3) | async-done | bytes 6291488 | tf_op jit(solution)/shard_map/all_to_all | solution.py:42
  491.5 96.1 %all_to_all.53 = bf16[64,48,640]{2,1,0:T(8,128)(2,1)S(1)} all-to-all(bf16[64,48,640]{2,1,0:T(8,128)(2,1)} %bitcast.55), channel_id=1, replica_groups=mesh['expert'=64,'tensor'=4] {'expert'}, dimensions={0} | all-to-all | bytes 7864320 | tf_op jit(solution)/shard_map/all_to_all | solution.py:26
  587.6 7.9 %fusion.12 = f32[1024,640]{0,1:T(8,128)S(1)} fusion(bf16[1024,3072]{1,0:T(8,128)(2,1)} %bitcast.8, bf16[3072,640]{1,0:T(8,128)(2,1)S(1)} %bitcast.53), kind=kOutput, calls=%fused_computation.28 | convolution fusion | flops 4026531840 | bytes 12845056 | tf_op jit(solution)/shard_map/dot_general | solution.py:44
  595.5 0.4 fusion.2
  595.9 1.2 copy.47
  597.1 6.2 all-to-all-start.4
  603.3 0.1 mul.35
  603.4 22.9 %all-to-all-done.4 = bf16[64,16,320]{2,1,0:T(8,128)(2,1)S(1)} async-done(((bf16[64,16,320]{2,1,0:T(8,128)(2,1)}), bf16[64,16,320]{2,1,0:T(8,128)(2,1)S(1)}, u32[]{:S(2)}, u32[]{:S(2)}) %all-to-all-start.4) | async-done | bytes 655392 | tf_op jit(solution)/shard_map/all_to_all | solution.py:51
  626.3 2.6 gather_fusion
  628.9 4.4 copy.55
  (20 shorter events, 0.2 us)
Async XLA Ops:
  0.6 172.1 %copy-start = (bf16[64,3072]{1,0:T(8,128)(2,1)S(1)}, bf16[64,3072]{1,0:T(8,128)(2,1)}, u32[]{:S(2)}) copy-start(bf16[64,3072]{1,0:T(8,128)(2,1)} %param.8) | copy-start | bytes 1179652
  154.9 15.0 %copy-start.3 = (s32[64,8]{0,1:T(8,128)S(1)}, s32[64,8]{0,1:T(8,128)}, u32[]{:S(2)}) copy-start(s32[64,8]{0,1:T(8,128)} %param.9) | copy-start | bytes 6148
  154.9 189.6 %all-to-all-start.1 = ((bf16[2,3072,640]{2,0,1:T(2,128)(2,1)}), bf16[2,3072,640]{2,0,1:T(2,128)(2,1)}, u32[]{:S(2)}, u32[]{:S(2)}) async-start(bf16[2,3072,640]{2,0,1:T(2,128)(2,1)} %reshape.123), calls=%async_computation.1 | async-start | bytes 15728640 | tf_op jit(solution)/shard_map/all_to_all | solution.py:22
  344.5 6.1 copy-start.4
  344.5 6.1 copy-start.5
  344.5 146.9 %all-to-all-start.3 = ((bf16[64,16,3072]{2,1,0:T(8,128)(2,1)}), bf16[64,16,3072]{2,1,0:T(8,128)(2,1)}, u32[]{:S(2)}, u32[]{:S(2)}) async-start(bf16[64,16,3072]{2,1,0:T(8,128)(2,1)} %bitcast.47), calls=%async_computation.3 | async-start | bytes 12582912 | tf_op jit(solution)/shard_map/all_to_all | solution.py:42
  587.6 7.9 %copy-start.2 = (bf16[64,48,640]{2,1,0:T(8,128)(2,1)}, bf16[64,48,640]{2,1,0:T(8,128)(2,1)S(1)}, u32[]{:S(2)}) copy-start(bf16[64,48,640]{2,1,0:T(8,128)(2,1)S(1)} %all_to_all.53) | copy-start | bytes 11796484
  597.1 36.1 %copy-start.1 = (bf16[64,3072]{1,0:T(8,128)(2,1)S(1)}, bf16[64,3072]{1,0:T(8,128)(2,1)}, u32[]{:S(2)}) copy-start(bf16[64,3072]{1,0:T(8,128)(2,1)} %param.8) | copy-start | bytes 1179652
  597.1 29.2 %all-to-all-start.4 = ((bf16[64,16,320]{2,1,0:T(8,128)(2,1)}), bf16[64,16,320]{2,1,0:T(8,128)(2,1)S(1)}, u32[]{:S(2)}, u32[]{:S(2)}) async-start(bf16[64,16,320]{2,1,0:T(8,128)(2,1)} %bitcast.10), calls=%async_computation.4 | async-start | bytes 1572864 | tf_op jit(solution)/shard_map/all_to_all | solution.py:51
where the time goes:
time: 635 us; the launch traced here: 633 us
  waiting for transfers between devices  314 us (49%)
  blocking collectives  187 us (29%)
  local copies, waits for them, and re-layouts  88.2 us (14%)
  starting transfers between devices  27.3 us (4%)
  matrix products  13.6 us (2%)
    all_to_all x1, waiting for transfers between devices, on_device(): lax.all_to_all(full_rows, 'expert', split_axis=1, concat_axis=0, tiled=True)  167 us
    all_to_all x1, waiting for transfers between devices, on_device(): lax.all_to_all(outgoing, 'expert', split_axis=0, concat_axis=0, tiled=True)  124 us
    all_to_all x1, blocking collectives, on_device(): lax.all_to_all(merged_rows, 'expert', split_axis=0, concat_axis=1, tiled=...  96.1 us
    all_to_all x1, blocking collectives, on_device(): lax.all_to_all(split_columns, 'tensor', split_axis=3, concat_axis=1, tile...  90.8 us
    reshape x2, local copies, waits for them, and re-layouts, on_device(): moved.reshape(local_members, local_rows * tensor_count, 2 * column_part)  49.1 us
    unnamed x17, local copies, waits for them, and re-layouts  23 us
    all_to_all x1, waiting for transfers between devices, on_device(): lax.all_to_all(activated, 'expert', split_axis=0, concat_axis=0, tiled=True)  22.9 us
    all_to_all x1, starting transfers between devices, on_device(): lax.all_to_all(full_rows, 'expert', split_axis=1, concat_axis=0, tiled=True)  15 us
  transfers between devices with their start and end apart: 3, of which 3 were waited for; matrix products, arithmetic and copies ran while one was open for 4% of the time, Pallas kernels for 0%

commit v1 on v0

v1 whole, which is shorter than its diff:
```python
import jax
import jax.numpy as jnp
from jax import lax
from jax.experimental import pallas as pl
from jax.experimental.pallas import tpu as pltpu
from jax.sharding import PartitionSpec as P

MESH = pl.DeviceIdType.MESH
CHUNKS = ((0, 0, 1), (0, 1, 2), (1, 0, 3), (2, 0, 3), (3, 0, 3), (4, 0, 2), (4, 2, 1))
NC = len(CHUNKS)
NX, NY, NZ, NP, CAP = 4, 4, 8, 8, 16
W1, W2 = 256, 128
BF = jnp.bfloat16
F32 = jnp.float32


def chunk_shapes():
    ys, yr, xr, zr, bs, br = [], [], [], [], [], []
    for _, _, nj in CHUNKS:
        r = 16 * nj
        ys.append((NY, 2, 2, NZ, r, 128))
        yr.append((NY, 2, 2, NZ, r, 128))
        xr.append((NP, 2, NZ, r, 128))
        zr.append((NZ, NP, 2, r, 128))
        bs.append((NZ, NP, r, 128))
        br.append((NP, NZ, r, 128))
    return ys, yr, xr, zr, bs, br


S_Y, S_X, S_Z, S_BZ, S_BX = 0, NC, 2 * NC, 3 * NC, 4 * NC
S_TZ = 5 * NC
S_SZ, S_TX, S_TY, S_H1X, S_H1Z, S_H2X, S_H2Z = (S_TZ + i for i in range(1, 8))
NS = S_TZ + 8
L_RAW, L_TOK, L_OUT, L_F = 0, 3, 4, 9
NL = 10


def half_tiles(b, t):
    found = []
    for h in range(2):
        col = b * 128 + h * 64
        raw = t * 320 + col if col < 320 else 1280 + t * 320 + col - 320
        found.append((raw // 128, (raw // 64) % 2))
    return found


def kernel(idx_ref, wgt_ref, w_hbm, tok_hbm, sel_ref, f_hbm, *refs):
    out_hbm, hid_ref = refs[0], refs[1]
    yr, xr, br = refs[2:2 + NC], refs[2 + NC:2 + 2 * NC], refs[2 + 2 * NC:2 + 3 * NC]
    refs = refs[2 + 3 * NC:]
    ys, zr, bs = refs[:NC], refs[NC:2 * NC], refs[2 * NC:3 * NC]
    (raw, wv, tsrc, tz, sz, tsel, tok, acc, act1, act2, hx1, hx2, hz1, hz2, f_ref, ssem, rsem, lsem) = refs[3 * NC:]
    e = lax.axis_index("expert")
    y = lax.axis_index("tensor")
    x, z, k = e // 16, (e // 2) % 8, e % 2
    p = x * 2 + k

    def at_y(t):
        return {"expert": e, "tensor": t}

    def at_z(t):
        return {"expert": x * 16 + t * 2 + k, "tensor": y}

    def at_p(t):
        return {"expert": (t // 2) * 16 + z * 2 + t % 2, "tensor": y}

    groups = ((NY, y, at_y), (NP, p, at_p), (NZ, z, at_z))

    raw_loads = []
    for j in range(3):
        rows = pl.ds(j * 16, 16)
        c = pltpu.make_async_copy(w_hbm.at[:, :, :, rows, :], raw.at[:, :, :, rows, :], lsem.at[L_RAW + j])
        c.start()
        raw_loads.append(c)
        if j == 0:
            tok_load = pltpu.make_async_copy(tok_hbm.at[:, pl.ds(pl.multiple_of(y * 768, 128), 768)], tsrc, lsem.at[L_TOK])
            tok_load.start()
    f_load = pltpu.make_async_copy(f_hbm, f_ref, lsem.at[L_F])
    f_load.start()

    barrier = pltpu.get_barrier_semaphore()
    for n, me, at in groups:
        def greet(d, carry, n=n, me=me, at=at):
            pl.semaphore_signal(barrier, inc=1, device_id=at((me + d) % n), device_id_type=MESH)
            return carry
        lax.fori_loop(1, n, greet, 0)
    pl.semaphore_wait(barrier, NY + NP + NZ - 3)

    drains = []

    def exchange(group, stage, source, target, own=True):
        n, me, at = groups[group]
        if own:
            pltpu.make_async_copy(source(me), target(me), rsem.at[stage]).start()

        def send(d, carry):
            t = (me + d) % n
            pltpu.make_async_remote_copy(
                src_ref=source(t), dst_ref=target(me), send_sem=ssem.at[stage], recv_sem=rsem.at[stage],
                device_id=at(t), device_id_type=MESH,
            ).start()
            return carry

        lax.fori_loop(1, n, send, 0)

    def wait_all(stage, ref):
        pltpu.make_async_copy(ref, ref, rsem.at[stage]).wait()

    def drain(stage, ref):
        drains.append((stage, ref))

    def relayout(c):
        b, j0, nj = CHUNKS[c]
        rows = pl.ds(j0 * 16, nj * 16)
        lane = lax.broadcasted_iota(jnp.int32, (nj * 16, 128), 1)

        def one(i, carry):
            m, kk, zz = i // 16, (i // 8) % 2, i % 8
            for t in range(NY):
                (lo, lo_half), (hi, hi_half) = half_tiles(b, t)
                if lo == hi:
                    ys[c][t, m, kk, zz] = raw[m, kk, zz, rows, lo * 128:lo * 128 + 128]
                    continue
                low = raw[m, kk, zz, rows, lo * 128:lo * 128 + 128].astype(F32)
                high = raw[m, kk, zz, rows, hi * 128:hi * 128 + 128].astype(F32)
                if lo_half == 1:
                    low = pltpu.roll(low, 64, 1)
                if hi_half == 0:
                    high = pltpu.roll(high, 64, 1)
                ys[c][t, m, kk, zz] = jnp.where(lane < 64, low, high).astype(BF)
            return carry

        lax.fori_loop(0, 32, one, 0)

    def stage_y(c):
        exchange(0, S_Y + c, lambda t: ys[c].at[t], lambda s: yr[c].at[s])
        drain(S_Y + c, yr[c].at[pl.ds(0, 3)])

    def stage_x(c):
        wait_all(S_Y + c, yr[c])
        exchange(1, S_X + c, lambda t: yr[c].at[t // 2, :, t % 2], lambda s: xr[c].at[s])
        drain(S_X + c, xr[c].at[pl.ds(0, 7)])

    def stage_z(c):
        wait_all(S_X + c, xr[c])
        exchange(2, S_Z + c, lambda t: xr[c].at[:, :, t], lambda s: zr[c].at[s])
        drain(S_Z + c, zr[c].at[pl.ds(0, 7)])

    def stage_bz(c):
        wait_all(S_Z + c, zr[c])

        def one(i, carry):
            total = None
            for m in range(4):
                where = idx_ref[i * 4 + m]
                term = zr[c][where >> 4, (where >> 1) & 7, where & 1].astype(F32) * wgt_ref[i * 4 + m]
                total = term if total is None else total + term
            bs[c][i // 8, i % 8] = total.astype(BF)
            return carry

        lax.fori_loop(0, 64, one, 0)
        exchange(2, S_BZ + c, lambda t: bs[c].at[t], lambda s: br[c].at[:, s])
        drain(S_BZ + c, br[c].at[pl.ds(0, 7)])

    def stage_bx(c):
        b, j0, nj = CHUNKS[c]
        wait_all(S_BZ + c, br[c])
        exchange(1, S_BX + c, lambda t: br[c].at[t],
                 lambda s: wv.at[b, pl.ds(s * 8, 8), pl.ds(j0 * 16, nj * 16)])
        drain(S_BX + c, wv.at[b, pl.ds(0, 56), pl.ds(j0 * 16, nj * 16)])

    out_copies = []

    def served(c):
        b, j0, nj = CHUNKS[c]
        wait_all(S_BX + c, wv.at[b, :, pl.ds(j0 * 16, nj * 16)])
        if j0 + nj < 3:
            return
        copy = pltpu.make_async_copy(wv.at[b], out_hbm.at[:, :, pl.ds(b * 128, 128)], lsem.at[L_OUT + b])
        copy.start()
        out_copies.append(copy)

        def rows_of(i, carry):
            total = None
            for q in range(NY):
                lhs = tok[q, pl.ds(i * 4, 4)].reshape(512, 768)
                rhs = wv[b, pl.ds(q * 16, 16)].reshape(768, 128)
                part = jnp.dot(lhs, rhs, preferred_element_type=F32)
                total = part if total is None else total + part
            acc[pl.ds(i * 512, 512), b * 128:b * 128 + 128] = total
            return carry

        lax.fori_loop(0, 2, rows_of, 0)

    def silu_up(gate, up):
        return (gate / (1.0 + jnp.exp(-gate))) * up

    def activate_first():
        def one(i, carry):
            r = pl.ds(i * 128, 128)
            hidden = silu_up(acc[r, 0:192], acc[r, 320:512]).astype(BF)
            act1[i] = jnp.concatenate([hidden, jnp.zeros((128, 64), BF)], axis=1).reshape(8, 16, W1)
            return carry

        lax.fori_loop(0, 8, one, 0)

    def activate_second():
        def one(i, carry):
            r = pl.ds(i * 128, 128)
            act2[i] = silu_up(acc[r, 192:320], acc[r, 512:640]).astype(BF).reshape(8, 16, W2)
            return carry

        lax.fori_loop(0, 8, one, 0)

    def hidden_x(stage, act, hx):
        exchange(1, stage, lambda t: act.at[t], lambda s: hx.at[s])
        drain(stage, hx.at[pl.ds(0, 7)])

    def hidden_z(before, stage, hx, hz):
        wait_all(before, hx)
        exchange(2, stage, lambda t: hx.at[:, t], lambda s: hz.at[s])
        drain(stage, hz.at[pl.ds(0, 7)])

    def tokens_z():
        tok_load.wait()
        exchange(2, S_SZ, lambda t: sel_ref.at[t], lambda s: sz.at[s])
        exchange(2, S_TZ, lambda t: tsrc, lambda s: tz.at[s])
        drain(S_SZ, sz.at[pl.ds(0, 7)])
        drain(S_TZ, tz.at[pl.ds(0, 7)])

    def tokens_x():
        wait_all(S_SZ, sz)
        wait_all(S_TZ, tz)

        def one(i, carry):
            chosen = jnp.dot(sz[i][:, 0:64], tz[i], preferred_element_type=F32).astype(BF)
            tsel[:, i] = chosen.reshape(8, 16, 768)
            return carry

        lax.fori_loop(0, 8, one, 0)
        exchange(1, S_TX, lambda t: tsel.at[t], lambda s: tok.at[y, s])
        drain(S_TX, tsel.at[pl.ds(0, 7)])

    def tokens_y():
        wait_all(S_TX, tok.at[y])
        exchange(0, S_TY, lambda t: tok.at[y], lambda s: tok.at[s], own=False)
        drain(S_TY, tok.at[pl.ds(0, 3)])

    def tokens_done():
        wait_all(S_TY, tok.at[pl.ds(0, 3)])

    raw_loads[0].wait()
    relayout(0)
    stage_y(0)
    tokens_z()
    raw_loads[1].wait()
    raw_loads[2].wait()
    relayout(1)
    stage_x(0)
    stage_y(1)
    relayout(2)
    stage_z(0)
    stage_x(1)
    stage_y(2)
    tokens_x()
    relayout(3)
    stage_z(1)
    tokens_y()
    for c in range(NC):
        if c + 2 < NC:
            stage_x(c + 2)
        if c + 3 < NC:
            stage_y(c + 3)
        if c + 4 < NC:
            relayout(c + 4)
        stage_bz(c)
        if c + 2 < NC:
            stage_z(c + 2)
        if c >= 1:
            stage_bx(c - 1)
        if c == 2:
            tokens_done()
        if c >= 2:
            served(c - 2)
    f_load.wait()
    stage_bx(NC - 1)
    served(NC - 2)
    activate_first()
    hidden_x(S_H1X, act1, hx1)
    hidden_z(S_H1X, S_H1Z, hx1, hz1)
    served(NC - 1)
    activate_second()
    hidden_x(S_H2X, act2, hx2)
    hidden_z(S_H2X, S_H2Z, hx2, hz2)

    def finish(hz, width, keep, at):
        got = jnp.dot(f_ref[...], hz[...].reshape(1024, width), preferred_element_type=F32)
        hid_ref[:, :, at:at + keep] = got[:, 0:keep].reshape(64, 8, keep).astype(BF)

    wait_all(S_H1Z, hz1)
    finish(hz1, W1, 192, 0)
    wait_all(S_H2Z, hz2)
    finish(hz2, W2, 128, 192)
    for copy in out_copies:
        copy.wait()
    for stage, ref in drains:
        pltpu.make_async_copy(ref, ref, ssem.at[stage]).wait()


def on_device(member_weights, cluster_ids, merge_counts, tokens, routes):
    member_count = cluster_ids.shape[0]
    cluster_count = 64
    ids = cluster_ids
    same = ids[None, :] == ids[:, None]
    earlier = jnp.arange(member_count)[None, :] < jnp.arange(member_count)[:, None]
    place = jnp.sum(same & earlier, axis=1)
    zz, pp = jnp.meshgrid(jnp.arange(8), jnp.arange(8), indexing="ij")
    cluster_of = ((pp // 2) * 16 + zz * 2 + pp % 2).reshape(-1)
    member = jnp.arange(member_count, dtype=jnp.int32)
    owner = member // 2
    encoded = ((owner // 2) % 8) * 16 + ((owner // 16) * 2 + owner % 2) * 2 + member % 2
    hit = (ids[None, None, :] == cluster_of[:, None, None]) & (place[None, None, :] == jnp.arange(4)[None, :, None])
    index_table = jnp.sum(jnp.where(hit, encoded, 0), axis=2).astype(jnp.int32)
    count_table = jnp.sum(jnp.where(hit, merge_counts, 0), axis=2).astype(F32)
    weight_table = count_table / jnp.sum(count_table, axis=1, keepdims=True)

    token_count, top = routes.shape
    named = jnp.any(routes[None, :, :] == jnp.arange(cluster_count)[:, None, None], axis=2)
    before = jnp.arange(token_count)[:, None] < jnp.arange(token_count)[None, :]
    rank = jnp.dot(named.astype(BF), before.astype(BF), preferred_element_type=F32).astype(jnp.int32)
    tagged = jnp.where(named, rank, -1)
    tagged = tagged.reshape(4, 8, 2, token_count).transpose(1, 0, 2, 3).reshape(cluster_count, 1, token_count)
    chosen = (tagged == jnp.arange(CAP)[None, :, None]).astype(BF).reshape(8, 128, token_count)
    selection = jnp.pad(chosen, ((0, 0), (0, 0), (0, 128 - token_count)))
    my_rank = jnp.sum(jnp.where(routes[:, :, None] == jnp.arange(cluster_count), rank.T[:, None, :], 0), axis=2)
    slot = ((routes // 2) % 8) * 128 + ((routes // 16) * 2 + routes % 2) * CAP + my_rank
    finder = (slot.reshape(-1, 1) == jnp.arange(1024)[None, :]).astype(BF)

    ys, yr, xr, zr, bs, br = chunk_shapes()
    hbm = pl.BlockSpec(memory_space=pltpu.HBM)
    vmem = pl.BlockSpec(memory_space=pltpu.VMEM)
    smem = pl.BlockSpec(memory_space=pltpu.SMEM)
    outs = [jax.ShapeDtypeStruct((64, 48, 640), BF), jax.ShapeDtypeStruct((64, 8, 320), BF)]
    outs += [jax.ShapeDtypeStruct(s, BF) for s in yr + xr + br]
    scratch = [pltpu.VMEM(s, BF) for s in ys + zr + bs]
    scratch += [
        pltpu.VMEM((2, 2, 8, 48, 2560), BF),
        pltpu.VMEM((5, 64, 48, 128), BF),
        pltpu.VMEM((64, 768), BF),
        pltpu.VMEM((8, 64, 768), BF),
        pltpu.VMEM((8, 128, 128), BF),
        pltpu.VMEM((8, 8, 16, 768), BF),
        pltpu.VMEM((4, 8, 8, 16, 768), BF),
        pltpu.VMEM((1024, 640), F32),
        pltpu.VMEM((8, 8, 16, W1), BF),
        pltpu.VMEM((8, 8, 16, W2), BF),
        pltpu.VMEM((8, 8, 16, W1), BF),
        pltpu.VMEM((8, 8, 16, W2), BF),
        pltpu.VMEM((8, 8, 16, W1), BF),
        pltpu.VMEM((8, 8, 16, W2), BF),
        pltpu.VMEM((512, 1024), BF),
        pltpu.SemaphoreType.DMA((NS,)),
        pltpu.SemaphoreType.DMA((NS,)),
        pltpu.SemaphoreType.DMA((NL,)),
    ]
    results = pl.pallas_call(
        kernel,
        out_shape=outs,
        in_specs=[smem, smem, hbm, hbm, vmem, hbm],
        out_specs=[hbm, vmem] + [hbm] * (3 * NC),
        scratch_shapes=scratch,
        compiler_params=pltpu.CompilerParams(collective_id=0, has_side_effects=True, vmem_limit_bytes=60 * 1024 * 1024),
    )(
        index_table.reshape(-1), weight_table.reshape(-1), member_weights.reshape(2, 2, 8, 48, 2560), tokens,
        selection, finder,
    )
    return results[0].reshape(1, 3072, 640), results[1]


def solution(mesh):
    return jax.shard_map(
        on_device,
        mesh=mesh,
        in_specs=(P("expert", "tensor", None), P(), P(), P("expert", None), P("expert", None)),
        out_specs=(P("expert", None, "tensor"), P("expert", None, "tensor")),
        check_vma=False,
    )
```

time: 635 us -> 388 us (0.61)
  Pallas kernels: 0 us -> 372 us
  waiting for transfers between devices: 314 us -> 0 us
  blocking collectives: 187 us -> 0 us
  local copies, waits for them, and re-layouts: 88.2 us -> 7.9 us
  starting transfers between devices: 27.3 us -> 0 us
  matrix products: 13.6 us -> 0.13 us
    pallas_call x0 -> x1, Pallas kernels: none -> 372 us  [on_device(): pl.pallas_call(kernel, out_shape=outs, in_specs=[smem, smem, hbm, hbm, vm...]
    all_to_all x3 -> x0, waiting for transfers between devices: 314 us -> none  [the longest x1 167 us: on_device(): lax.all_to_all(full_rows, 'expert', split_axis=1, concat_axis=0, tiled=True)]
    all_to_all x2 -> x0, blocking collectives: 187 us -> none  [the longest x1 96.1 us: on_device(): lax.all_to_all(merged_rows, 'expert', split_axis=0, concat_axis=1, tiled=...]
    reshape x3 -> x2, local copies, waits for them, and re-layouts: 52.8 us -> 0.71 us  [the longest x1 0.7 us: on_device(): index_table.reshape(-1)]
    all_to_all x3 -> x0, starting transfers between devices: 27.3 us -> none  [the longest x1 15 us: on_device(): lax.all_to_all(full_rows, 'expert', split_axis=1, concat_axis=0, tiled=True)]
    unnamed x17 -> x5, local copies, waits for them, and re-layouts: 23 us -> 5.94 us
    dot_general x3 -> x1, matrix products: 13.6 us -> 0.13 us  [on_device(): jnp.dot(named.astype(BF), before.astype(BF), preferred_element_type=F32)]
    all_to_all x2 -> x0, local copies, waits for them, and re-layouts: 8.07 us -> none  [on_device(): lax.all_to_all(full_rows, 'expert', split_axis=1, concat_axis=0, tiled=True)]
  transfers between devices with their start and end apart: 3 -> 0, of which waited for: 3 -> 0; matrix products, arithmetic and copies ran while one was open for 4% -> 0% of each run, Pallas kernels for 0% -> 0%
where the time goes in v1:
time: 388 us
  Pallas kernels  372 us (96%)
  local copies, waits for them, and re-layouts  7.9 us (2%)
  other arithmetic  6.89 us (2%)
    pallas_call x1, Pallas kernels, on_device(): pl.pallas_call(kernel, out_shape=outs, in_specs=[smem, smem, hbm, hbm, vm...  372 us

profile of v1, /device:TPU:1, one launch (start us, length us, event | category | flops | bytes accessed | tf_op | source)
XLA Modules:
  0.0 387.7 jit_solution(17225937876274646696)
XLA Ops:
  0.6 0.9 convert_reduce_fusion
  1.6 0.1 add_add_fusion
  1.7 0.1 reshape.164
  1.8 0.1 eq.137
  1.9 0.7 broadcast_compare_fusion
  2.6 0.9 fusion.3
  3.5 0.8 fusion.1
  4.3 0.1 copy.16
  4.4 0.7 div.74.wgt_ref
  5.1 0.1 copy.15
  5.2 0.7 reshape.159.idx_ref
  5.9 0.8 copy.18
  6.6 0.1 broadcast_select_fusion
  6.8 0.1 copy.23
  6.9 1.3 select_reduce_fusion
  8.1 0.1 fusion.8
  8.2 0.1 eq.143
  8.3 0.1 bitcast_compare_fusion
  8.5 0.8 pad_convert_fusion.sel_ref
  9.3 1.2 fusion.f_hbm
  10.5 372.1 %shard_map.68 = (bf16[64,48,640]{2,1,0:T(8,128)(2,1)}, bf16[64,8,320]{2,1,0:T(8,128)(2,1)}, bf16[4,2,2,8,16,128]{5,4,3,2,1,0:T(8,128)(2,1)}, bf16[4,2,2,8,32,128...) custom-call(s32[256]{0:T(256)} %reshape.159.idx_ref, ...), custom_call_target="tpu_custom_call" | custom-call | tf_op jit(solution)/shard_map/pallas_call | solution.py:366
  382.6 0.0 copy-start
  382.6 4.4 %copy.26 = bf16[1,3072,640]{2,1,0:T(8,128)(2,1)} copy(bf16[1,3072,640]{2,1,0:T(8,128)(2,1)} %bitcast.12) | data formatting | bytes 7864320
  387.0 0.0 copy-done
  387.0 0.7 copy.27
  (11 shorter events, 0.1 us)
Async XLA Ops:
  382.6 4.4 %copy-start = (bf16[64,8,320]{2,1,0:T(8,128)(2,1)S(1)}, bf16[64,8,320]{2,1,0:T(8,128)(2,1)}, u32[]{:S(2)}) copy-start(bf16[64,8,320]{2,1,0:T(8,128)(2,1)} %get-tuple-element.19) | copy-start | bytes 983044

commit v2 on v1

--- a/solution.py
+++ b/solution.py
@@ -6,7 +6,13 @@
 from jax.sharding import PartitionSpec as P
 
 MESH = pl.DeviceIdType.MESH
-CHUNKS = ((0, 0, 1), (0, 1, 2), (1, 0, 3), (2, 0, 3), (3, 0, 3), (4, 0, 2), (4, 2, 1))
+CHUNKS = ((0, 0, 1), (0, 1, 1), (0, 2, 1), (1, 0, 3), (2, 0, 3), (3, 0, 3), (4, 0, 1), (4, 1, 1), (4, 2, 1))
+ORDER = (
+    "TZ", "Y0", "Y1", "X0", "Y2", "Y3", "X1", "Z0", "TX", "X2", "Z1", "E0", "E1", "Y4", "B0", "Y8", "Y7", "X3", "Z2",
+    "B1", "E2", "Z3", "X4", "Y6", "X8", "Z4", "G1", "Y5", "X5", "B2", "E3", "X7", "TY", "Z5", "E4", "E5", "B3", "B4",
+    "B5", "G2", "Z7", "G0", "Z8", "G3", "G4", "X6", "S1", "S2", "E7", "Z6", "G5", "S0", "S3", "E8", "B7", "E6", "H",
+    "B8", "B6", "G7", "G8", "I", "G6", "S4", "J", "K",
+)
 NC = len(CHUNKS)
 NX, NY, NZ, NP, CAP = 4, 4, 8, 8, 16
 W1, W2 = 256, 128
@@ -15,20 +21,22 @@
 
 
 def chunk_shapes():
-    ys, yr, xr, zr, bs, br = [], [], [], [], [], []
+    ys, yr, xr, zr, es, er, bs, br = [], [], [], [], [], [], [], []
     for _, _, nj in CHUNKS:
         r = 16 * nj
         ys.append((NY, 2, 2, NZ, r, 128))
         yr.append((NY, 2, 2, NZ, r, 128))
         xr.append((NP, 2, NZ, r, 128))
-        zr.append((NZ, NP, 2, r, 128))
-        bs.append((NZ, NP, r, 128))
+        zr.append((2, 4, NP, 2, r, 128))
+        es.append((2, 4, NP, r, 128))
+        er.append((2, 4, NP, r, 128))
+        bs.append((2, 4, NP, r, 128))
         br.append((NP, NZ, r, 128))
-    return ys, yr, xr, zr, bs, br
-
-
-S_Y, S_X, S_Z, S_BZ, S_BX = 0, NC, 2 * NC, 3 * NC, 4 * NC
-S_TZ = 5 * NC
+    return ys, yr, xr, zr, es, er, bs, br
+
+
+S_Y, S_X, S_Z, S_E, S_BZ, S_BX = 0, NC, 2 * NC, 3 * NC, 4 * NC, 5 * NC
+S_TZ = 6 * NC
 S_SZ, S_TX, S_TY, S_H1X, S_H1Z, S_H2X, S_H2Z = (S_TZ + i for i in range(1, 8))
 NS = S_TZ + 8
 L_RAW, L_TOK, L_OUT, L_F = 0, 3, 4, 9
@@ -48,8 +56,8 @@
     out_hbm, hid_ref = refs[0], refs[1]
     yr, xr, br = refs[2:2 + NC], refs[2 + NC:2 + 2 * NC], refs[2 + 2 * NC:2 + 3 * NC]
     refs = refs[2 + 3 * NC:]
-    ys, zr, bs = refs[:NC], refs[NC:2 * NC], refs[2 * NC:3 * NC]
-    (raw, wv, tsrc, tz, sz, tsel, tok, acc, act1, act2, hx1, hx2, hz1, hz2, f_ref, ssem, rsem, lsem) = refs[3 * NC:]
+    ys, zr, es, er, bs = (refs[i * NC:(i + 1) * NC] for i in range(5))
+    (raw, wv, tsrc, tz, sz, tsel, tok, acc, act1, act2, hx1, hx2, hz1, hz2, f_ref, ssem, rsem, lsem) = refs[5 * NC:]
     e = lax.axis_index("expert")
     y = lax.axis_index("tensor")
     x, z, k = e // 16, (e // 2) % 8, e % 2
@@ -141,26 +149,66 @@
         exchange(1, S_X + c, lambda t: yr[c].at[t // 2, :, t % 2], lambda s: xr[c].at[s])
         drain(S_X + c, xr[c].at[pl.ds(0, 7)])
 
+    def send_z(stage, source, target, there):
+        pltpu.make_async_remote_copy(
+            src_ref=source, dst_ref=target, send_sem=ssem.at[stage], recv_sem=rsem.at[stage],
+            device_id=at_z(there), device_id_type=MESH,
+        ).start()
+
     def stage_z(c):
         wait_all(S_X + c, xr[c])
-        exchange(2, S_Z + c, lambda t: xr[c].at[:, :, t], lambda s: zr[c].at[s])
-        drain(S_Z + c, zr[c].at[pl.ds(0, 7)])
+        pltpu.make_async_copy(xr[c].at[:, :, z], zr[c].at[0, 0], rsem.at[S_Z + c]).start()
+        pltpu.make_async_copy(xr[c].at[:, :, (z + 7) % 8], zr[c].at[1, 0], rsem.at[S_Z + c]).start()
+
+        def send(o, carry):
+            send_z(S_Z + c, xr[c].at[:, :, (z + o) % 8], zr[c].at[0, o], (z + o) % 8)
+            send_z(S_Z + c, xr[c].at[:, :, (z + 7 - o) % 8], zr[c].at[1, o], (z + 8 - o) % 8)
+            return carry
+
+        lax.fori_loop(1, 4, send, 0)
+        drain(S_Z + c, zr[c].at[:, pl.ds(0, 3)])
+
+    def weighted(c, role, entry):
+        total = None
+        for m in range(4):
+            where = idx_ref[entry + m]
+            term = zr[c][role, where >> 4, (where >> 1) & 7, where & 1].astype(F32) * wgt_ref[entry + m]
+            total = term if total is None else total + term
+        return total
+
+    def stage_e(c):
+        wait_all(S_Z + c, zr[c])
+
+        def one(i, carry):
+            es[c][i // 32, (i // 8) % 4, i % 8] = weighted(c, i // 32, i * 4).astype(BF)
+            return carry
+
+        lax.fori_loop(0, 64, one, 0)
+        send_z(S_E + c, es[c].at[0], er[c].at[1], (z + 1) % 8)
+        send_z(S_E + c, es[c].at[1], er[c].at[0], (z + 7) % 8)
+        drain(S_E + c, er[c])
 
     def stage_bz(c):
-        wait_all(S_Z + c, zr[c])
-
-        def one(i, carry):
-            total = None
-            for m in range(4):
-                where = idx_ref[i * 4 + m]
-                term = zr[c][where >> 4, (where >> 1) & 7, where & 1].astype(F32) * wgt_ref[i * 4 + m]
-                total = term if total is None else total + term
-            bs[c][i // 8, i % 8] = total.astype(BF)
+        wait_all(S_E + c, er[c])
+
+        def one(i, carry):
+            role, plane, owner = i // 32, (i // 8) % 4, i % 8
+            total = weighted(c, role, 256 + i * 4) + er[c][role, plane, owner].astype(F32)
+            bs[c][role, plane, owner] = total.astype(BF)
             return carry
 
         lax.fori_loop(0, 64, one, 0)
-        exchange(2, S_BZ + c, lambda t: bs[c].at[t], lambda s: br[c].at[:, s])
-        drain(S_BZ + c, br[c].at[pl.ds(0, 7)])
+        low = (z + 7) % 8
+        pltpu.make_async_copy(bs[c].at[0, 0], br[c].at[:, z], rsem.at[S_BZ + c]).start()
+        pltpu.make_async_copy(bs[c].at[1, 0], br[c].at[:, low], rsem.at[S_BZ + c]).start()
+
+        def send(o, carry):
+            send_z(S_BZ + c, bs[c].at[0, o], br[c].at[:, z], (z + 8 - o) % 8)
+            send_z(S_BZ + c, bs[c].at[1, o], br[c].at[:, low], (z + o) % 8)
+            return carry
+
+        lax.fori_loop(1, 4, send, 0)
+        drain(S_BZ + c, br[c].at[pl.ds(0, 6)])
 
     def stage_bx(c):
         b, j0, nj = CHUNKS[c]
@@ -171,11 +219,15 @@
 
     out_copies = []
 
-    def served(c):
-        b, j0, nj = CHUNKS[c]
-        wait_all(S_BX + c, wv.at[b, :, pl.ds(j0 * 16, nj * 16)])
-        if j0 + nj < 3:
-            return
+    ready = []
+
+    def served(b):
+        if not ready:
+            tokens_done()
+            ready.append(True)
+        for c, (block, j0, nj) in enumerate(CHUNKS):
+            if block == b:
+                wait_all(S_BX + c, wv.at[b, :, pl.ds(j0 * 16, nj * 16)])
         copy = pltpu.make_async_copy(wv.at[b], out_hbm.at[:, :, pl.ds(b * 128, 128)], lsem.at[L_OUT + b])
         copy.start()
         out_copies.append(copy)
@@ -249,49 +301,36 @@
     def tokens_done():
         wait_all(S_TY, tok.at[pl.ds(0, 3)])
 
-    raw_loads[0].wait()
-    relayout(0)
-    stage_y(0)
-    tokens_z()
-    raw_loads[1].wait()
-    raw_loads[2].wait()
-    relayout(1)
-    stage_x(0)
-    stage_y(1)
-    relayout(2)
-    stage_z(0)
-    stage_x(1)
-    stage_y(2)
-    tokens_x()
-    relayout(3)
-    stage_z(1)
-    tokens_y()
-    for c in range(NC):
-        if c + 2 < NC:
-            stage_x(c + 2)
-        if c + 3 < NC:
-            stage_y(c + 3)
-        if c + 4 < NC:
-            relayout(c + 4)
-        stage_bz(c)
-        if c + 2 < NC:
-            stage_z(c + 2)
-        if c >= 1:
-            stage_bx(c - 1)
-        if c == 2:
-            tokens_done()
-        if c >= 2:
-            served(c - 2)
+    loaded = set()
+
+    def first(c):
+        b, j0, nj = CHUNKS[c]
+        for j in range(j0, j0 + nj):
+            if j not in loaded:
+                loaded.add(j)
+                raw_loads[j].wait()
+        relayout(c)
+        stage_y(c)
+
+    def third():
+        activate_first()
+        hidden_x(S_H1X, act1, hx1)
+
+    def fourth():
+        activate_second()
+        hidden_x(S_H2X, act2, hx2)
+
+    stages = {"Y": first, "X": stage_x, "Z": stage_z, "E": stage_e, "B": stage_bz, "G": stage_bx, "S": served}
+    once = {
+        "TZ": tokens_z, "TX": tokens_x, "TY": tokens_y, "H": third, "J": fourth,
+        "I": lambda: hidden_z(S_H1X, S_H1Z, hx1, hz1), "K": lambda: hidden_z(S_H2X, S_H2Z, hx2, hz2),
+    }
+    for step in ORDER:
+        if step in once:
+            once[step]()
+        else:
+            stages[step[0]](int(step[1:]))
     f_load.wait()
-    stage_bx(NC - 1)
-    served(NC - 2)
-    activate_first()
-    hidden_x(S_H1X, act1, hx1)
-    hidden_z(S_H1X, S_H1Z, hx1, hz1)
-    served(NC - 1)
-    activate_second()
-    hidden_x(S_H2X, act2, hx2)
-    hidden_z(S_H2X, S_H2Z, hx2, hz2)
 
     def finish(hz, width, keep, at):
         got = jnp.dot(f_ref[...], hz[...].reshape(1024, width), preferred_element_type=F32)
@@ -310,19 +349,22 @@
 def on_device(member_weights, cluster_ids, merge_counts, tokens, routes):
     member_count = cluster_ids.shape[0]
     cluster_count = 64
-    ids = cluster_ids
-    same = ids[None, :] == ids[:, None]
-    earlier = jnp.arange(member_count)[None, :] < jnp.arange(member_count)[:, None]
-    place = jnp.sum(same & earlier, axis=1)
-    zz, pp = jnp.meshgrid(jnp.arange(8), jnp.arange(8), indexing="ij")
-    cluster_of = ((pp // 2) * 16 + zz * 2 + pp % 2).reshape(-1)
+    z = (lax.axis_index("expert") // 2) % 8
+    same = cluster_ids[None, :] == cluster_ids[:, None]
     member = jnp.arange(member_count, dtype=jnp.int32)
+    place = jnp.sum(same & (member[None, :] < member[:, None]), axis=1)
+    weight = merge_counts.astype(F32) / jnp.sum(jnp.where(same, merge_counts[None, :], 0), axis=1).astype(F32)
+    entry = jnp.arange(512, dtype=jnp.int32)
+    own, role, i, p, m = entry // 256, (entry // 128) % 2, (entry // 32) % 4, (entry // 4) % 8, entry % 4
+    plane = jnp.where(role == 0, jnp.where(own == 1, z - i, z + 1 + i), jnp.where(own == 1, z + i, z - 1 - i)) % 8
+    cluster_of = (p // 2) * 16 + plane * 2 + p % 2
     owner = member // 2
-    encoded = ((owner // 2) % 8) * 16 + ((owner // 16) * 2 + owner % 2) * 2 + member % 2
-    hit = (ids[None, None, :] == cluster_of[:, None, None]) & (place[None, None, :] == jnp.arange(4)[None, :, None])
-    index_table = jnp.sum(jnp.where(hit, encoded, 0), axis=2).astype(jnp.int32)
-    count_table = jnp.sum(jnp.where(hit, merge_counts, 0), axis=2).astype(F32)
-    weight_table = count_table / jnp.sum(count_table, axis=1, keepdims=True)
+    away = (z - (owner // 2) % 8) % 8
+    away = jnp.where(role[:, None] == 0, away[None, :], ((8 - away) % 8)[None, :])
+    hit = (cluster_ids[None, :] == cluster_of[:, None]) & (place[None, :] == m[:, None]) & (away < 4)
+    inside = ((owner // 16) * 2 + owner % 2) * 2 + member % 2
+    index_table = jnp.sum(jnp.where(hit, away * 16 + inside[None, :], 0), axis=1).astype(jnp.int32)
+    weight_table = jnp.sum(jnp.where(hit, weight[None, :], 0.0), axis=1)
 
     token_count, top = routes.shape
     named = jnp.any(routes[None, :, :] == jnp.arange(cluster_count)[:, None, None], axis=2)
@@ -336,13 +378,13 @@
     slot = ((routes // 2) % 8) * 128 + ((routes // 16) * 2 + routes % 2) * CAP + my_rank
     finder = (slot.reshape(-1, 1) == jnp.arange(1024)[None, :]).astype(BF)
 
-    ys, yr, xr, zr, bs, br = chunk_shapes()
+    ys, yr, xr, zr, es, er, bs, br = chunk_shapes()
     hbm = pl.BlockSpec(memory_space=pltpu.HBM)
     vmem = pl.BlockSpec(memory_space=pltpu.VMEM)
     smem = pl.BlockSpec(memory_space=pltpu.SMEM)
     outs = [jax.ShapeDtypeStruct((64, 48, 640), BF), jax.ShapeDtypeStruct((64, 8, 320), BF)]
     outs += [jax.ShapeDtypeStruct(s, BF) for s in yr + xr + br]
-    scratch = [pltpu.VMEM(s, BF) for s in ys + zr + bs]
+    scratch = [pltpu.VMEM(s, BF) for s in ys + zr + es + er + bs]
     scratch += [
         pltpu.VMEM((2, 2, 8, 48, 2560), BF),
         pltpu.VMEM((5, 64, 48, 128), BF),
@@ -371,7 +413,7 @@
         scratch_shapes=scratch,
         compiler_params=pltpu.CompilerParams(collective_id=0, has_side_effects=True, vmem_limit_bytes=60 * 1024 * 1024),
     )(
-        index_table.reshape(-1), weight_table.reshape(-1), member_weights.reshape(2, 2, 8, 48, 2560), tokens,
+        index_table, weight_table, member_weights.reshape(2, 2, 8, 48, 2560), tokens,
         selection, finder,
     )
     return results[0].reshape(1, 3072, 640), results[1]

time: 388 us -> 324 us (0.84)
  Pallas kernels: 372 us -> 306 us
    pallas_call x1, Pallas kernels: 372 us -> 306 us  [on_device(): pl.pallas_call(kernel, out_shape=outs, in_specs=[smem, smem, hbm, hbm, vm...]
where the time goes in v2:
time: 324 us; the launch traced here: 323 us
  Pallas kernels  306 us (94%)
  other arithmetic  9.1 us (3%)
  local copies, waits for them, and re-layouts  6.24 us (2%)
    pallas_call x1, Pallas kernels, on_device(): pl.pallas_call(kernel, out_shape=outs, in_specs=[smem, smem, hbm, hbm, vm...  306 us

profile of v2, /device:TPU:1, one launch (start us, length us, event | category | flops | bytes accessed | tf_op | source)
XLA Modules:
  0.0 322.6 jit_solution(3967423053567624838)
XLA Ops:
  0.7 0.9 fusion.6
  1.6 0.7 convert_divide_fusion
  2.3 1.6 select_reduce_fusion.1.wgt_ref
  3.9 1.6 fusion.3.idx_ref
  5.6 0.1 eq.164
  5.6 0.8 fusion.4
  6.4 0.8 copy.16
  7.2 0.1 broadcast_select_fusion
  7.3 0.1 copy.21
  7.4 1.3 select_reduce_fusion
  8.7 0.1 fusion.10
  8.8 0.1 eq.170
  8.9 0.1 bitcast_compare_fusion
  9.0 0.8 pad_convert_fusion.sel_ref
  9.8 1.2 fusion.f_hbm
  11.0 306.4 %shard_map.68 = (bf16[64,48,640]{2,1,0:T(8,128)(2,1)}, bf16[64,8,320]{2,1,0:T(8,128)(2,1)}, bf16[4,2,2,8,16,128]{5,4,3,2,1,0:T(8,128)(2,1)}, bf16[4,2,2,8,16,128...) custom-call(s32[512]{0:T(512)} %fusion.3.idx_ref, ...), custom_call_target="tpu_custom_call" | custom-call | tf_op jit(solution)/shard_map/pallas_call | solution.py:408
  317.4 0.0 copy-start
  317.5 4.4 %copy.24 = bf16[1,3072,640]{2,1,0:T(8,128)(2,1)} copy(bf16[1,3072,640]{2,1,0:T(8,128)(2,1)} %bitcast.12) | data formatting | bytes 7864320
  321.9 0.0 copy-done
  321.9 0.7 copy.25
  (7 shorter events, 0.1 us)
Async XLA Ops:
  317.4 4.4 %copy-start = (bf16[64,8,320]{2,1,0:T(8,128)(2,1)S(1)}, bf16[64,8,320]{2,1,0:T(8,128)(2,1)}, u32[]{:S(2)}) copy-start(bf16[64,8,320]{2,1,0:T(8,128)(2,1)} %get-tuple-element.17) | copy-start | bytes 983044

commit v3 on v2

--- a/solution.py
+++ b/solution.py
@@ -8,10 +8,10 @@
 MESH = pl.DeviceIdType.MESH
 CHUNKS = ((0, 0, 1), (0, 1, 1), (0, 2, 1), (1, 0, 3), (2, 0, 3), (3, 0, 3), (4, 0, 1), (4, 1, 1), (4, 2, 1))
 ORDER = (
-    "TZ", "Y0", "Y1", "X0", "Y2", "Y3", "X1", "Z0", "TX", "X2", "Z1", "E0", "E1", "Y4", "B0", "Y8", "Y7", "X3", "Z2",
-    "B1", "E2", "Z3", "X4", "Y6", "X8", "Z4", "G1", "Y5", "X5", "B2", "E3", "X7", "TY", "Z5", "E4", "E5", "B3", "B4",
-    "B5", "G2", "Z7", "G0", "Z8", "G3", "G4", "X6", "S1", "S2", "E7", "Z6", "G5", "S0", "S3", "E8", "B7", "E6", "H",
-    "B8", "B6", "G7", "G8", "I", "G6", "S4", "J", "K",
+    "Y1", "TZ", "Y2", "Y7", "X1", "X2", "Y0", "Z1", "Y5", "Y3", "X7", "Z2", "M", "E1", "Y4", "X0", "Z7", "Z0", "B1",
+    "X5", "Y8", "E2", "E7", "E0", "Z5", "X3", "Y6", "G1", "X4", "Z3", "E5", "B2", "Z4", "TX", "TY", "T", "E3", "X8",
+    "B5", "B0", "G2", "E4", "B3", "X6", "Z8", "G0", "B4", "G5", "S3", "G3", "S0", "Z6", "G4", "E8", "S1", "B7", "E6",
+    "B8", "S2", "H", "B6", "G7", "G8", "I", "G6", "S4", "J", "K",
 )
 NC = len(CHUNKS)
 NX, NY, NZ, NP, CAP = 4, 4, 8, 8, 16
@@ -39,8 +39,8 @@
 S_TZ = 6 * NC
 S_SZ, S_TX, S_TY, S_H1X, S_H1Z, S_H2X, S_H2Z = (S_TZ + i for i in range(1, 8))
 NS = S_TZ + 8
-L_RAW, L_TOK, L_OUT, L_F = 0, 3, 4, 9
-NL = 10
+L_RAW, L_TOK, L_OUT, L_TAB = 0, 3, 4, 9
+NL = 11
 
 
 def half_tiles(b, t):
@@ -52,12 +52,13 @@
     return found
 
 
-def kernel(idx_ref, wgt_ref, w_hbm, tok_hbm, sel_ref, f_hbm, *refs):
+def kernel(ids_ref, cnt_ref, routes_ref, w_hbm, tok_hbm, *refs):
     out_hbm, hid_ref = refs[0], refs[1]
     yr, xr, br = refs[2:2 + NC], refs[2 + NC:2 + 2 * NC], refs[2 + 2 * NC:2 + 3 * NC]
     refs = refs[2 + 3 * NC:]
     ys, zr, es, er, bs = (refs[i * NC:(i + 1) * NC] for i in range(5))
-    (raw, wv, tsrc, tz, sz, tsel, tok, acc, act1, act2, hx1, hx2, hz1, hz2, f_ref, ssem, rsem, lsem) = refs[5 * NC:]
+    (raw, wv, tsrc, tz, sz, tsel, tok, acc, act1, act2, hx1, hx2, hz1, hz2, f_ref,
+     f_tmp, sel_ref, idx_vmem, wgt_vmem, idx_ref, wgt_ref, ssem, rsem, lsem) = refs[5 * NC:]
     e = lax.axis_index("expert")
     y = lax.axis_index("tensor")
     x, z, k = e // 16, (e // 2) % 8, e % 2
@@ -83,16 +84,14 @@
         if j == 0:
             tok_load = pltpu.make_async_copy(tok_hbm.at[:, pl.ds(pl.multiple_of(y * 768, 128), 768)], tsrc, lsem.at[L_TOK])
             tok_load.start()
-    f_load = pltpu.make_async_copy(f_hbm, f_ref, lsem.at[L_F])
-    f_load.start()
-
     barrier = pltpu.get_barrier_semaphore()
     for n, me, at in groups:
         def greet(d, carry, n=n, me=me, at=at):
             pl.semaphore_signal(barrier, inc=1, device_id=at((me + d) % n), device_id_type=MESH)
             return carry
         lax.fori_loop(1, n, greet, 0)
-    pl.semaphore_wait(barrier, NY + NP + NZ - 3)
+    def iota(rows, columns, axis):
+        return lax.broadcasted_iota(jnp.int32, (rows, columns), axis)
 
     drains = []
 
@@ -171,8 +170,8 @@
     def weighted(c, role, entry):
         total = None
         for m in range(4):
-            where = idx_ref[entry + m]
-            term = zr[c][role, where >> 4, (where >> 1) & 7, where & 1].astype(F32) * wgt_ref[entry + m]
+            where = idx_ref[0, entry + m]
+            term = zr[c][role, (where >> 4) & 3, (where >> 1) & 7, where & 1].astype(F32) * wgt_ref[0, entry + m]
             total = term if total is None else total + term
         return total
 
@@ -283,9 +282,13 @@
     def tokens_x():
         wait_all(S_SZ, sz)
         wait_all(S_TZ, tz)
-
-        def one(i, carry):
-            chosen = jnp.dot(sz[i][:, 0:64], tz[i], preferred_element_type=F32).astype(BF)
+        repeat = jnp.where((iota(128, 16, 0) >> 4) == iota(128, 16, 1), 1.0, 0.0).astype(BF)
+        slot = (iota(128, 128, 0) & 15).astype(F32)
+
+        def one(i, carry):
+            ranks = jnp.dot(repeat, sz[i], preferred_element_type=F32)
+            pick = jnp.where(ranks == slot, 1.0, 0.0)[:, 0:64].astype(BF)
+            chosen = jnp.dot(pick, tz[i], preferred_element_type=F32).astype(BF)
             tsel[:, i] = chosen.reshape(8, 16, 768)
             return carry
 
@@ -301,7 +304,71 @@
     def tokens_done():
         wait_all(S_TY, tok.at[pl.ds(0, 3)])
 
+    def merge_tables():
+        ids, counts = ids_ref[...], cnt_ref[...]
+        row, column = iota(128, 128, 0), iota(128, 128, 1)
+        ids_down = jnp.sum(jnp.where(row == column, ids, 0), axis=1, keepdims=True)
+        counts_down = jnp.sum(jnp.where(row == column, counts, 0), axis=1, keepdims=True)
+        same = ids_down == ids
+        place = jnp.sum(jnp.where(same & (column < row), 1, 0), axis=1, keepdims=True)
+        total = jnp.sum(jnp.where(same, counts, 0), axis=1, keepdims=True)
+        weight = counts_down.astype(F32) / total.astype(F32)
+        member = iota(128, 512, 0)
+        owner = member >> 1
+        plane_of = (owner >> 1) & 7
+        inside = ((owner >> 4) * 2 + (owner & 1)) * 2 + (member & 1)
+        entry = iota(128, 512, 1)
+        own, role, i, q, m = entry >> 8, (entry >> 7) & 1, (entry >> 5) & 3, (entry >> 2) & 7, entry & 3
+        plane = jnp.where(role == 0, jnp.where(own == 1, z - i, z + 1 + i), jnp.where(own == 1, z + i, z - 1 - i)) & 7
+        cluster = (q >> 1) * 16 + plane * 2 + (q & 1)
+        away = jnp.where(role == 0, z - plane_of, plane_of - z) & 7
+        hit = (ids_down == cluster) & (place == m) & (away < 4)
+        idx_vmem[...] = jnp.sum(jnp.where(hit, away * 16 + inside, 0), axis=0, keepdims=True)
+        wgt_vmem[...] = jnp.sum(jnp.where(hit, weight, 0.0), axis=0, keepdims=True)
+        pltpu.make_async_copy(idx_vmem, idx_ref, lsem.at[L_TAB]).start()
+        pltpu.make_async_copy(wgt_vmem, wgt_ref, lsem.at[L_TAB + 1]).start()
+
+    def merge_tables_done():
+        pltpu.make_async_copy(idx_vmem, idx_ref, lsem.at[L_TAB]).wait()
+        pltpu.make_async_copy(wgt_vmem, wgt_ref, lsem.at[L_TAB + 1]).wait()
+
+    def slot_ranks():
+        routes = routes_ref[...]
+        hits = [jnp.where(routes[:, j:j + 1] == iota(64, 64, 1), 1.0, 0.0) for j in range(8)]
+        named = sum(hits[1:], hits[0])
+        lower = jnp.where(iota(64, 64, 1) < iota(64, 64, 0), 1.0, 0.0).astype(BF)
+        rank = jnp.dot(lower, named.astype(BF), preferred_element_type=F32)
+        return routes, hits, named, rank
+
+    def select_tokens():
+        routes, hits, named, rank = slot_ranks()
+        tagged = jnp.where(named > 0.0, rank, -1.0)
+        tagged = jnp.concatenate([tagged, jnp.full((64, 64), -1.0, F32)], axis=0).astype(BF)
+        unit = jnp.where(iota(64, 64, 0) == iota(64, 64, 1), 1.0, 0.0).astype(BF)
+        across = lax.dot_general(unit, tagged, (((1,), (1,)), ((), ())), preferred_element_type=F32).astype(BF)
+        row = iota(128, 64, 0)
+        cluster = ((row & 15) >> 1) * 16 + (row >> 4) * 2 + (row & 1)
+        spread = jnp.where(cluster == iota(128, 64, 1), 1.0, 0.0).astype(BF)
+        sel_ref[...] = jnp.dot(spread, across, preferred_element_type=F32).astype(BF).reshape(8, 16, 128)
+
+    def find_slots():
+        routes, hits, named, rank = slot_ranks()
+        for j in range(8):
+            mine = jnp.sum(hits[j] * rank, axis=1, keepdims=True).astype(jnp.int32)
+            r = routes[:, j:j + 1]
+            slot = ((r >> 1) & 7) * 128 + ((r >> 4) * 2 + (r & 1)) * CAP + mine
+            f_tmp[j * 64:j * 64 + 64, :] = jnp.where(slot == iota(64, 1024, 1), 1.0, 0.0).astype(BF)
+
+        def one(i, carry):
+            row = iota(128, 512, 0) + i * 128
+            order = jnp.where(iota(128, 512, 1) == (row & 7) * 64 + (row >> 3), 1.0, 0.0).astype(BF)
+            f_ref[pl.ds(i * 128, 128), :] = jnp.dot(order, f_tmp[...], preferred_element_type=F32).astype(BF)
+            return carry
+
+        lax.fori_loop(0, 4, one, 0)
+
     loaded = set()
+    early = set()
 
     def first(c):
         b, j0, nj = CHUNKS[c]
@@ -309,7 +376,8 @@
             if j not in loaded:
                 loaded.add(j)
                 raw_loads[j].wait()
-        relayout(c)
+        if c not in early:
+            relayout(c)
         stage_y(c)
 
     def third():
@@ -322,15 +390,21 @@
 
     stages = {"Y": first, "X": stage_x, "Z": stage_z, "E": stage_e, "B": stage_bz, "G": stage_bx, "S": served}
     once = {
-        "TZ": tokens_z, "TX": tokens_x, "TY": tokens_y, "H": third, "J": fourth,
+        "M": merge_tables_done, "T": find_slots, "TZ": tokens_z, "TX": tokens_x, "TY": tokens_y, "H": third, "J": fourth,
         "I": lambda: hidden_z(S_H1X, S_H1Z, hx1, hz1), "K": lambda: hidden_z(S_H2X, S_H2Z, hx2, hz2),
     }
+    merge_tables()
+    select_tokens()
+    raw_loads[0].wait()
+    loaded.add(0)
+    relayout(0)
+    early.add(0)
+    pl.semaphore_wait(barrier, NY + NP + NZ - 3)
     for step in ORDER:
         if step in once:
             once[step]()
         else:
             stages[step[0]](int(step[1:]))
-    f_load.wait()
 
     def finish(hz, width, keep, at):
         got = jnp.dot(f_ref[...], hz[...].reshape(1024, width), preferred_element_type=F32)
@@ -347,41 +421,9 @@
 
 
 def on_device(member_weights, cluster_ids, merge_counts, tokens, routes):
-    member_count = cluster_ids.shape[0]
-    cluster_count = 64
-    z = (lax.axis_index("expert") // 2) % 8
-    same = cluster_ids[None, :] == cluster_ids[:, None]
-    member = jnp.arange(member_count, dtype=jnp.int32)
-    place = jnp.sum(same & (member[None, :] < member[:, None]), axis=1)
-    weight = merge_counts.astype(F32) / jnp.sum(jnp.where(same, merge_counts[None, :], 0), axis=1).astype(F32)
-    entry = jnp.arange(512, dtype=jnp.int32)
-    own, role, i, p, m = entry // 256, (entry // 128) % 2, (entry // 32) % 4, (entry // 4) % 8, entry % 4
-    plane = jnp.where(role == 0, jnp.where(own == 1, z - i, z + 1 + i), jnp.where(own == 1, z + i, z - 1 - i)) % 8
-    cluster_of = (p // 2) * 16 + plane * 2 + p % 2
-    owner = member // 2
-    away = (z - (owner // 2) % 8) % 8
-    away = jnp.where(role[:, None] == 0, away[None, :], ((8 - away) % 8)[None, :])
-    hit = (cluster_ids[None, :] == cluster_of[:, None]) & (place[None, :] == m[:, None]) & (away < 4)
-    inside = ((owner // 16) * 2 + owner % 2) * 2 + member % 2
-    index_table = jnp.sum(jnp.where(hit, away * 16 + inside[None, :], 0), axis=1).astype(jnp.int32)
-    weight_table = jnp.sum(jnp.where(hit, weight[None, :], 0.0), axis=1)
-
-    token_count, top = routes.shape
-    named = jnp.any(routes[None, :, :] == jnp.arange(cluster_count)[:, None, None], axis=2)
-    before = jnp.arange(token_count)[:, None] < jnp.arange(token_count)[None, :]
-    rank = jnp.dot(named.astype(BF), before.astype(BF), preferred_element_type=F32).astype(jnp.int32)
-    tagged = jnp.where(named, rank, -1)
-    tagged = tagged.reshape(4, 8, 2, token_count).transpose(1, 0, 2, 3).reshape(cluster_count, 1, token_count)
-    chosen = (tagged == jnp.arange(CAP)[None, :, None]).astype(BF).reshape(8, 128, token_count)
-    selection = jnp.pad(chosen, ((0, 0), (0, 0), (0, 128 - token_count)))
-    my_rank = jnp.sum(jnp.where(routes[:, :, None] == jnp.arange(cluster_count), rank.T[:, None, :], 0), axis=2)
-    slot = ((routes // 2) % 8) * 128 + ((routes // 16) * 2 + routes % 2) * CAP + my_rank
-    finder = (slot.reshape(-1, 1) == jnp.arange(1024)[None, :]).astype(BF)
-
     ys, yr, xr, zr, es, er, bs, br = chunk_shapes()
     hbm = pl.BlockSpec(memory_space=pltpu.HBM)
     vmem = pl.BlockSpec(memory_space=pltpu.VMEM)
-    smem = pl.BlockSpec(memory_space=pltpu.SMEM)
     outs = [jax.ShapeDtypeStruct((64, 48, 640), BF), jax.ShapeDtypeStruct((64, 8, 320), BF)]
     outs += [jax.ShapeDtypeStruct(s, BF) for s in yr + xr + br]
     scratch = [pltpu.VMEM(s, BF) for s in ys + zr + es + er + bs]
@@ -390,7 +432,7 @@
         pltpu.VMEM((5, 64, 48, 128), BF),
         pltpu.VMEM((64, 768), BF),
         pltpu.VMEM((8, 64, 768), BF),
-        pltpu.VMEM((8, 128, 128), BF),
+        pltpu.VMEM((8, 16, 128), BF),
         pltpu.VMEM((8, 8, 16, 768), BF),
         pltpu.VMEM((4, 8, 8, 16, 768), BF),
         pltpu.VMEM((1024, 640), F32),
@@ -401,6 +443,12 @@
         pltpu.VMEM((8, 8, 16, W1), BF),
         pltpu.VMEM((8, 8, 16, W2), BF),
         pltpu.VMEM((512, 1024), BF),
+        pltpu.VMEM((512, 1024), BF),
+        pltpu.VMEM((8, 16, 128), BF),
+        pltpu.VMEM((1, 512), jnp.int32),
+        pltpu.VMEM((1, 512), F32),
+        pltpu.SMEM((1, 512), jnp.int32),
+        pltpu.SMEM((1, 512), F32),
         pltpu.SemaphoreType.DMA((NS,)),
         pltpu.SemaphoreType.DMA((NS,)),
         pltpu.SemaphoreType.DMA((NL,)),
@@ -408,13 +456,12 @@
     results = pl.pallas_call(
         kernel,
         out_shape=outs,
-        in_specs=[smem, smem, hbm, hbm, vmem, hbm],
+        in_specs=[vmem, vmem, vmem, hbm, hbm],
         out_specs=[hbm, vmem] + [hbm] * (3 * NC),
         scratch_shapes=scratch,
         compiler_params=pltpu.CompilerParams(collective_id=0, has_side_effects=True, vmem_limit_bytes=60 * 1024 * 1024),
     )(
-        index_table, weight_table, member_weights.reshape(2, 2, 8, 48, 2560), tokens,
-        selection, finder,
+        cluster_ids.reshape(1, -1), merge_counts.reshape(1, -1), routes, member_weights.reshape(2, 2, 8, 48, 2560), tokens,
     )
     return results[0].reshape(1, 3072, 640), results[1]
 

time: 324 us -> 302 us (0.932)
  Pallas kernels: 306 us -> 294 us
  other arithmetic: 9.1 us -> 0 us
    pallas_call x1, Pallas kernels: 306 us -> 294 us  [on_device(): pl.pallas_call(kernel, out_shape=outs, in_specs=[vmem, vmem, vmem, hbm, h...]
    reduce_sum x4 -> x0, other arithmetic: 5.38 us -> none  [the longest x1 1.62 us: on_device(): jnp.sum(jnp.where(hit, away * 16 + inside[None, :], 0), axis=1)]
where the time goes in v3:
time: 302 us
  Pallas kernels  294 us (97%)
  local copies, waits for them, and re-layouts  6.56 us (2%)
    pallas_call x1, Pallas kernels, on_device(): pl.pallas_call(kernel, out_shape=outs, in_specs=[vmem, vmem, vmem, hbm, h...  294 us
    unnamed x5, local copies, waits for them, and re-layouts  6.56 us

profile of v3, /device:TPU:1, one launch (start us, length us, event | category | flops | bytes accessed | tf_op | source)
XLA Modules:
  0.0 301.5 jit_solution(10193849633468931052)
XLA Ops:
  0.6 1.4 copy.7.routes_ref
  2.0 294.3 %shard_map.68 = (bf16[64,48,640]{2,1,0:T(8,128)(2,1)}, bf16[64,8,320]{2,1,0:T(8,128)(2,1)}, bf16[4,2,2,8,16,128]{5,4,3,2,1,0:T(8,128)(2,1)}, bf16[4,2,2,8,16,128...) custom-call(s32[1,128]{1,0:T(1,128)} %bitcast.6, ...), custom_call_target="tpu_custom_call" | custom-call | tf_op jit(solution)/shard_map/pallas_call | solution.py:456
  296.3 0.0 copy-start
  296.3 4.4 %copy.10 = bf16[1,3072,640]{2,1,0:T(8,128)(2,1)} copy(bf16[1,3072,640]{2,1,0:T(8,128)(2,1)} %bitcast.5) | data formatting | bytes 7864320
  300.8 0.0 copy-done
  300.8 0.7 copy.11
Async XLA Ops:
  296.3 4.4 %copy-start = (bf16[64,8,320]{2,1,0:T(8,128)(2,1)S(1)}, bf16[64,8,320]{2,1,0:T(8,128)(2,1)}, u32[]{:S(2)}) copy-start(bf16[64,8,320]{2,1,0:T(8,128)(2,1)} %get-tuple-element.9) | copy-start | bytes 983044

commit v4 on v3

--- a/solution.py
+++ b/solution.py
@@ -37,10 +37,10 @@
 
 S_Y, S_X, S_Z, S_E, S_BZ, S_BX = 0, NC, 2 * NC, 3 * NC, 4 * NC, 5 * NC
 S_TZ = 6 * NC
-S_SZ, S_TX, S_TY, S_H1X, S_H1Z, S_H2X, S_H2Z = (S_TZ + i for i in range(1, 8))
-NS = S_TZ + 8
-L_RAW, L_TOK, L_OUT, L_TAB = 0, 3, 4, 9
-NL = 11
+S_SZ, S_TX, S_TY, S_H1X, S_H1Z, S_H1B, S_H2X, S_H2Z = (S_TZ + i for i in range(1, 9))
+NS = S_TZ + 9
+L_RAW, L_TOK, L_OUT, L_TAB, L_F = 0, 3, 4, 9, 11
+NL = 12
 
 
 def half_tiles(b, t):
@@ -53,11 +53,11 @@
 
 
 def kernel(ids_ref, cnt_ref, routes_ref, w_hbm, tok_hbm, *refs):
-    out_hbm, hid_ref = refs[0], refs[1]
-    yr, xr, br = refs[2:2 + NC], refs[2 + NC:2 + 2 * NC], refs[2 + 2 * NC:2 + 3 * NC]
-    refs = refs[2 + 3 * NC:]
+    out_hbm, f_hbm, hz1, hz1b, hz2 = refs[:5]
+    yr, xr, br = (refs[5 + i * NC:5 + (i + 1) * NC] for i in range(3))
+    refs = refs[5 + 3 * NC:]
     ys, zr, es, er, bs = (refs[i * NC:(i + 1) * NC] for i in range(5))
-    (raw, wv, tsrc, tz, sz, tsel, tok, acc, act1, act2, hx1, hx2, hz1, hz2, f_ref,
+    (raw, wv, tsrc, tz, sz, tsel, tok, acc, act1, act2, hx1, hx2, pack, f_ref,
      f_tmp, sel_ref, idx_vmem, wgt_vmem, idx_ref, wgt_ref, ssem, rsem, lsem) = refs[5 * NC:]
     e = lax.axis_index("expert")
     y = lax.axis_index("tensor")
@@ -227,7 +227,7 @@
         for c, (block, j0, nj) in enumerate(CHUNKS):
             if block == b:
                 wait_all(S_BX + c, wv.at[b, :, pl.ds(j0 * 16, nj * 16)])
-        copy = pltpu.make_async_copy(wv.at[b], out_hbm.at[:, :, pl.ds(b * 128, 128)], lsem.at[L_OUT + b])
+        copy = pltpu.make_async_copy(wv.at[b], out_hbm.at[b], lsem.at[L_OUT + b])
         copy.start()
         out_copies.append(copy)
 
@@ -267,10 +267,25 @@
         exchange(1, stage, lambda t: act.at[t], lambda s: hx.at[s])
         drain(stage, hx.at[pl.ds(0, 7)])
 
-    def hidden_z(before, stage, hx, hz):
-        wait_all(before, hx)
-        exchange(2, stage, lambda t: hx.at[:, t], lambda s: hz.at[s])
-        drain(stage, hz.at[pl.ds(0, 7)])
+    def hidden_z_first():
+        wait_all(S_H1X, hx1)
+        lanes = pl.ds(0, 128)
+        exchange(2, S_H1Z, lambda t: hx1.at[:, t, :, lanes], lambda s: hz1.at[s])
+        drain(S_H1Z, hz1.at[pl.ds(0, 7)])
+
+        def one(i, carry):
+            t, q = i // 4, i % 4
+            pack[t, q] = jnp.concatenate([hx1[q, t, :, 128:192], hx1[q + 4, t, :, 128:192]], axis=1)
+            return carry
+
+        lax.fori_loop(0, 32, one, 0)
+        exchange(2, S_H1B, lambda t: pack.at[t], lambda s: hz1b.at[s])
+        drain(S_H1B, hz1b.at[pl.ds(0, 7)])
+
+    def hidden_z_second():
+        wait_all(S_H2X, hx2)
+        exchange(2, S_H2Z, lambda t: hx2.at[:, t], lambda s: hz2.at[s])
+        drain(S_H2Z, hz2.at[pl.ds(0, 7)])
 
     def tokens_z():
         tok_load.wait()
@@ -333,7 +348,9 @@
         pltpu.make_async_copy(wgt_vmem, wgt_ref, lsem.at[L_TAB + 1]).wait()
 
     def slot_ranks():
-        routes = routes_ref[...]
+        unit = jnp.where(iota(64, 64, 0) == iota(64, 64, 1), 1.0, 0.0).astype(BF)
+        turned = routes_ref[...].astype(F32).astype(BF)
+        routes = lax.dot_general(unit, turned, (((1,), (1,)), ((), ())), preferred_element_type=F32).astype(jnp.int32)
         hits = [jnp.where(routes[:, j:j + 1] == iota(64, 64, 1), 1.0, 0.0) for j in range(8)]
         named = sum(hits[1:], hits[0])
         lower = jnp.where(iota(64, 64, 1) < iota(64, 64, 0), 1.0, 0.0).astype(BF)
@@ -366,6 +383,9 @@
             return carry
 
         lax.fori_loop(0, 4, one, 0)
+        copy = pltpu.make_async_copy(f_ref, f_hbm, lsem.at[L_F])
+        copy.start()
+        out_copies.append(copy)
 
     loaded = set()
     early = set()
@@ -391,14 +411,16 @@
     stages = {"Y": first, "X": stage_x, "Z": stage_z, "E": stage_e, "B": stage_bz, "G": stage_bx, "S": served}
     once = {
         "M": merge_tables_done, "T": find_slots, "TZ": tokens_z, "TX": tokens_x, "TY": tokens_y, "H": third, "J": fourth,
-        "I": lambda: hidden_z(S_H1X, S_H1Z, hx1, hz1), "K": lambda: hidden_z(S_H2X, S_H2Z, hx2, hz2),
+        "I": hidden_z_first, "K": hidden_z_second,
     }
     merge_tables()
     select_tokens()
-    raw_loads[0].wait()
-    loaded.add(0)
-    relayout(0)
-    early.add(0)
+    opening = int(next(step for step in ORDER if step[0] == "Y")[1:])
+    for j in range(CHUNKS[opening][1], CHUNKS[opening][1] + CHUNKS[opening][2]):
+        raw_loads[j].wait()
+        loaded.add(j)
+    relayout(opening)
+    early.add(opening)
     pl.semaphore_wait(barrier, NY + NP + NZ - 3)
     for step in ORDER:
         if step in once:
@@ -406,25 +428,43 @@
         else:
             stages[step[0]](int(step[1:]))
 
-    def finish(hz, width, keep, at):
-        got = jnp.dot(f_ref[...], hz[...].reshape(1024, width), preferred_element_type=F32)
-        hid_ref[:, :, at:at + keep] = got[:, 0:keep].reshape(64, 8, keep).astype(BF)
-
     wait_all(S_H1Z, hz1)
-    finish(hz1, W1, 192, 0)
+    wait_all(S_H1B, hz1b)
     wait_all(S_H2Z, hz2)
-    finish(hz2, W2, 128, 192)
     for copy in out_copies:
         copy.wait()
     for stage, ref in drains:
         pltpu.make_async_copy(ref, ref, ssem.at[stage]).wait()
 
 
+def place_results(blocks, f_ref, first_ref, tail_ref, last_ref, out_hbm, hid_ref, held, load_sem, store_sem):
+    loads, stores = [], []
+    for b in range(5):
+        loads.append(pltpu.make_async_copy(blocks.at[b], held.at[b], load_sem.at[b]))
+        stores.append(pltpu.make_async_copy(held.at[b], out_hbm.at[:, :, pl.ds(b * 128, 128)], store_sem.at[b]))
+        loads[b].start()
+
+    def find(rows):
+        return jnp.dot(f_ref[...], rows, preferred_element_type=F32)
+
+    tail = tail_ref[...]
+    tail = jnp.concatenate([tail[:, :, :, 0:64], tail[:, :, :, 64:128]], axis=1).reshape(1024, 64)
+    hid_ref[:, :, 0:128] = find(first_ref[...].reshape(1024, 128)).reshape(64, 8, 128).astype(BF)
+    for b in range(5):
+        loads[b].wait()
+        stores[b].start()
+    hid_ref[:, :, 128:192] = find(tail).reshape(64, 8, 64).astype(BF)
+    hid_ref[:, :, 192:320] = find(last_ref[...].reshape(1024, 128)).reshape(64, 8, 128).astype(BF)
+    for b in range(5):
+        stores[b].wait()
+
+
 def on_device(member_weights, cluster_ids, merge_counts, tokens, routes):
     ys, yr, xr, zr, es, er, bs, br = chunk_shapes()
     hbm = pl.BlockSpec(memory_space=pltpu.HBM)
     vmem = pl.BlockSpec(memory_space=pltpu.VMEM)
-    outs = [jax.ShapeDtypeStruct((64, 48, 640), BF), jax.ShapeDtypeStruct((64, 8, 320), BF)]
+    outs = [jax.ShapeDtypeStruct(s, BF) for s in (
+        (5, 64, 48, 128), (512, 1024), (8, 8, 16, 128), (8, 4, 16, 128), (8, 8, 16, 128))]
     outs += [jax.ShapeDtypeStruct(s, BF) for s in yr + xr + br]
     scratch = [pltpu.VMEM(s, BF) for s in ys + zr + es + er + bs]
     scratch += [
@@ -440,8 +480,7 @@
         pltpu.VMEM((8, 8, 16, W2), BF),
         pltpu.VMEM((8, 8, 16, W1), BF),
         pltpu.VMEM((8, 8, 16, W2), BF),
-        pltpu.VMEM((8, 8, 16, W1), BF),
-        pltpu.VMEM((8, 8, 16, W2), BF),
+        pltpu.VMEM((8, 4, 16, 128), BF),
         pltpu.VMEM((512, 1024), BF),
         pltpu.VMEM((512, 1024), BF),
         pltpu.VMEM((8, 16, 128), BF),
@@ -457,13 +496,21 @@
         kernel,
         out_shape=outs,
         in_specs=[vmem, vmem, vmem, hbm, hbm],
-        out_specs=[hbm, vmem] + [hbm] * (3 * NC),
+        out_specs=[hbm] * (5 + 3 * NC),
         scratch_shapes=scratch,
         compiler_params=pltpu.CompilerParams(collective_id=0, has_side_effects=True, vmem_limit_bytes=60 * 1024 * 1024),
     )(
-        cluster_ids.reshape(1, -1), merge_counts.reshape(1, -1), routes, member_weights.reshape(2, 2, 8, 48, 2560), tokens,
+        cluster_ids.reshape(1, -1), merge_counts.reshape(1, -1), routes.T, member_weights.reshape(2, 2, 8, 48, 2560), tokens,
     )
-    return results[0].reshape(1, 3072, 640), results[1]
+    merged, hidden = pl.pallas_call(
+        place_results,
+        out_shape=[jax.ShapeDtypeStruct((64, 48, 640), BF), jax.ShapeDtypeStruct((64, 8, 320), BF)],
+        in_specs=[hbm, vmem, vmem, vmem, vmem],
+        out_specs=[hbm, vmem],
+        scratch_shapes=[pltpu.VMEM((5, 64, 48, 128), BF), pltpu.SemaphoreType.DMA((5,)), pltpu.SemaphoreType.DMA((5,))],
+        compiler_params=pltpu.CompilerParams(vmem_limit_bytes=60 * 1024 * 1024),
+    )(*results[:5])
+    return merged.reshape(1, 3072, 640), hidden
 
 
 def solution(mesh):

time: 302 us -> 296 us (0.980)
  local copies, waits for them, and re-layouts: 6.56 us -> 0 us
    unnamed x5 -> x0, local copies, waits for them, and re-layouts: 6.56 us -> none
    pallas_call x0 -> x1, Pallas kernels: none -> 5.27 us  [on_device(): pl.pallas_call(place_results, out_shape=[jax.ShapeDtypeStruct((64, 48, 64...]
    pallas_call x1, Pallas kernels: 294 us -> 290 us  [on_device(): pl.pallas_call(kernel, out_shape=outs, in_specs=[vmem, vmem, vmem, hbm, h...]
where the time goes in v4:
time: 296 us
  Pallas kernels  295 us (100%)
    pallas_call x1, Pallas kernels, on_device(): pl.pallas_call(kernel, out_shape=outs, in_specs=[vmem, vmem, vmem, hbm, h...  290 us

profile of v4, /device:TPU:1, one launch (start us, length us, event | category | flops | bytes accessed | tf_op | source)
XLA Modules:
  0.0 296.0 jit_solution(4418081072277133298)
XLA Ops:
  0.6 290.1 %shard_map.68 = (bf16[5,64,48,128]{3,2,1,0:T(8,128)(2,1)}, bf16[512,1024]{1,0:T(8,128)(2,1)}, bf16[8,8,16,128]{3,2,1,0:T(8,128)(2,1)}, bf16[8,4,16,128]{3,2,1,0:...) custom-call(s32[1,128]{1,0:T(1,128)} %bitcast.7, ...), custom_call_target="tpu_custom_call" | custom-call | tf_op jit(solution)/shard_map/pallas_call | solution.py:495
  290.7 5.3 %shard_map.69 = (bf16[64,48,640]{2,1,0:T(8,128)(2,1)}, bf16[64,8,320]{2,1,0:T(8,128)(2,1)}) custom-call(bf16[5,64,48,128]{3,2,1,0:T(8,128)(2,1)} %get-tuple-element.9.blocks, bf16[512,1024]{1,0:T(8,128)(2,1)} %get-tuple-element.10.f_ref, bf16[8,8,16,128]{3,2,1,0:T(8,128)(2,1)} %get-tuple-element.11.first_ref, ...), custom_call_target="tpu_custom_call" | custom-call | tf_op jit(solution)/shard_map/pallas_call | solution.py:505

commit v5 on v4

--- a/solution.py
+++ b/solution.py
@@ -8,7 +8,7 @@
 MESH = pl.DeviceIdType.MESH
 CHUNKS = ((0, 0, 1), (0, 1, 1), (0, 2, 1), (1, 0, 3), (2, 0, 3), (3, 0, 3), (4, 0, 1), (4, 1, 1), (4, 2, 1))
 ORDER = (
-    "Y1", "TZ", "Y2", "Y7", "X1", "X2", "Y0", "Z1", "Y5", "Y3", "X7", "Z2", "M", "E1", "Y4", "X0", "Z7", "Z0", "B1",
+    "Y1", "TZ", "Y2", "Y7", "U", "X1", "X2", "Y0", "Z1", "Y5", "Y3", "X7", "Z2", "M", "E1", "Y4", "X0", "Z7", "Z0", "B1",
     "X5", "Y8", "E2", "E7", "E0", "Z5", "X3", "Y6", "G1", "X4", "Z3", "E5", "B2", "Z4", "TX", "TY", "T", "E3", "X8",
     "B5", "B0", "G2", "E4", "B3", "X6", "Z8", "G0", "B4", "G5", "S3", "G3", "S0", "Z6", "G4", "E8", "S1", "B7", "E6",
     "B8", "S2", "H", "B6", "G7", "G8", "I", "G6", "S4", "J", "K",
@@ -159,7 +159,8 @@
         pltpu.make_async_copy(xr[c].at[:, :, z], zr[c].at[0, 0], rsem.at[S_Z + c]).start()
         pltpu.make_async_copy(xr[c].at[:, :, (z + 7) % 8], zr[c].at[1, 0], rsem.at[S_Z + c]).start()
 
-        def send(o, carry):
+        def send(i, carry):
+            o = 4 - i
             send_z(S_Z + c, xr[c].at[:, :, (z + o) % 8], zr[c].at[0, o], (z + o) % 8)
             send_z(S_Z + c, xr[c].at[:, :, (z + 7 - o) % 8], zr[c].at[1, o], (z + 8 - o) % 8)
             return carry
@@ -201,7 +202,8 @@
         pltpu.make_async_copy(bs[c].at[0, 0], br[c].at[:, z], rsem.at[S_BZ + c]).start()
         pltpu.make_async_copy(bs[c].at[1, 0], br[c].at[:, low], rsem.at[S_BZ + c]).start()
 
-        def send(o, carry):
+        def send(i, carry):
+            o = 4 - i
             send_z(S_BZ + c, bs[c].at[0, o], br[c].at[:, z], (z + 8 - o) % 8)
             send_z(S_BZ + c, bs[c].at[1, o], br[c].at[:, low], (z + o) % 8)
             return carry
@@ -289,8 +291,9 @@
 
     def tokens_z():
         tok_load.wait()
+        exchange(2, S_TZ, lambda t: tsrc, lambda s: tz.at[s])
+        select_tokens()
         exchange(2, S_SZ, lambda t: sel_ref.at[t], lambda s: sz.at[s])
-        exchange(2, S_TZ, lambda t: tsrc, lambda s: tz.at[s])
         drain(S_SZ, sz.at[pl.ds(0, 7)])
         drain(S_TZ, tz.at[pl.ds(0, 7)])
 
@@ -410,11 +413,9 @@
 
     stages = {"Y": first, "X": stage_x, "Z": stage_z, "E": stage_e, "B": stage_bz, "G": stage_bx, "S": served}
     once = {
-        "M": merge_tables_done, "T": find_slots, "TZ": tokens_z, "TX": tokens_x, "TY": tokens_y, "H": third, "J": fourth,
+        "U": merge_tables, "M": merge_tables_done, "T": find_slots, "TZ": tokens_z, "TX": tokens_x, "TY": tokens_y, "H": third, "J": fourth,
         "I": hidden_z_first, "K": hidden_z_second,
     }
-    merge_tables()
-    select_tokens()
     opening = int(next(step for step in ORDER if step[0] == "Y")[1:])
     for j in range(CHUNKS[opening][1], CHUNKS[opening][1] + CHUNKS[opening][2]):
         raw_loads[j].wait()
@@ -447,12 +448,12 @@
     def find(rows):
         return jnp.dot(f_ref[...], rows, preferred_element_type=F32)
 
+    for b in range(5):
+        loads[b].wait()
+        stores[b].start()
     tail = tail_ref[...]
     tail = jnp.concatenate([tail[:, :, :, 0:64], tail[:, :, :, 64:128]], axis=1).reshape(1024, 64)
     hid_ref[:, :, 0:128] = find(first_ref[...].reshape(1024, 128)).reshape(64, 8, 128).astype(BF)
-    for b in range(5):
-        loads[b].wait()
-        stores[b].start()
     hid_ref[:, :, 128:192] = find(tail).reshape(64, 8, 64).astype(BF)
     hid_ref[:, :, 192:320] = find(last_ref[...].reshape(1024, 128)).reshape(64, 8, 128).astype(BF)
     for b in range(5):

time: 296 us -> 296 us (level)
  no operation moved by 1% of the time
where the time goes in v5:
time: 296 us; the launch traced here: 294 us
  Pallas kernels  294 us (99%)
    pallas_call x1, Pallas kernels, on_device(): pl.pallas_call(kernel, out_shape=outs, in_specs=[vmem, vmem, vmem, hbm, h...  288 us

profile of v5, /device:TPU:1, one launch (start us, length us, event | category | flops | bytes accessed | tf_op | source)
XLA Modules:
  0.0 294.3 jit_solution(9982870515958080025)
XLA Ops:
  0.6 288.3 %shard_map.68 = (bf16[5,64,48,128]{3,2,1,0:T(8,128)(2,1)}, bf16[512,1024]{1,0:T(8,128)(2,1)}, bf16[8,8,16,128]{3,2,1,0:T(8,128)(2,1)}, bf16[8,4,16,128]{3,2,1,0:...) custom-call(s32[1,128]{1,0:T(1,128)} %bitcast.7, ...), custom_call_target="tpu_custom_call" | custom-call | tf_op jit(solution)/shard_map/pallas_call | solution.py:496
  288.9 5.4 %shard_map.69 = (bf16[64,48,640]{2,1,0:T(8,128)(2,1)}, bf16[64,8,320]{2,1,0:T(8,128)(2,1)}) custom-call(bf16[5,64,48,128]{3,2,1,0:T(8,128)(2,1)} %get-tuple-element.9.blocks, bf16[512,1024]{1,0:T(8,128)(2,1)} %get-tuple-element.10.f_ref, bf16[8,8,16,128]{3,2,1,0:T(8,128)(2,1)} %get-tuple-element.11.first_ref, ...), custom_call_target="tpu_custom_call" | custom-call | tf_op jit(solution)/shard_map/pallas_call | solution.py:506
